TPU v7x, 32 devices: a whole 2x2x4 slice. The times are simulated.
32 devices in a mesh: row: 16 (over z, x, core), col: 2 (over y).
Axes of the slice: x: 2, y: 2, z: 4, core: 2. Of those that a mesh axis runs over, the one named last changes fastest.
Arguments:
- amplitudes: float32 [2, 16, 2, 262144], P(None, 'row', 'col'), may hold values from -6 to 6
- gate_matrices: float32 [5, 4, 2, 128, 128], replicated, may hold values from -0.375 to 0.375
- permutation: int32 [16], replicated, may hold values from 0 to 15, each once
Outputs:
- evolved: float32 [2, 16, 2, 262144], P(None, 'row', 'col')
Inputs may be any that keep to these rules, and one draw needn't show every extreme that they name: `permutation`: each value from 0 to 15 appears once.
All inputs are finite; a program needn't handle non-finite values.
Results may differ from a plain program's by a relative error of at most 0.00014.
Values sent between devices are 32-bit elements; how exact they have to be, the bound alone decides.
A program may use at most 64 MiB of HBM per device.

v0:
```python
import jax
import jax.numpy as jnp
from jax import lax
from jax.sharding import PartitionSpec as P

HIGHEST = lax.Precision.HIGHEST
GATE_KINDS = ("top", "mid", "low", "top")


def partner(value, axis, apart):
    mask = 2**apart
    pairs = [(source, source ^ mask) for source in range(lax.axis_size(axis))]
    return lax.ppermute(value, axis, pairs)


def stacked(gate_mat):
    real_part = gate_mat[0]
    imag_part = gate_mat[1]
    top_rows = jnp.concatenate([real_part, -imag_part], axis=1)
    bottom_rows = jnp.concatenate([imag_part, real_part], axis=1)
    return jnp.concatenate([top_rows, bottom_rows], axis=0)


def apply_gate(amp_flat, gate_mat, kind):
    gate_size = gate_mat.shape[-1]
    real_form = stacked(gate_mat)
    amp_count = amp_flat.shape[-1]
    if kind == "top":
        flattened = amp_flat.reshape(2 * gate_size, amp_count // gate_size)
        return jnp.dot(
            real_form, flattened, precision=HIGHEST, preferred_element_type=jnp.float32
        ).reshape(2, amp_count)
    real_quad = real_form.reshape(2, gate_size, 2, gate_size)
    if kind == "mid":
        blocks = amp_flat.reshape(2, amp_count // (gate_size * gate_size), gate_size, gate_size)
        return jnp.einsum("djck,cakb->dajb", real_quad, blocks, precision=HIGHEST).reshape(
            2, amp_count
        )
    columns = amp_flat.reshape(2, amp_count // gate_size, gate_size)
    return jnp.einsum("djck,cmk->dmj", real_quad, columns, precision=HIGHEST).reshape(2, amp_count)


def top_half(amp_flat, gate_mat, half_index):
    gate_size = gate_mat.shape[-1]
    amp_count = amp_flat.shape[-1]
    real_form = stacked(gate_mat).reshape(2, 2, gate_size // 2, 2 * gate_size)
    chosen = lax.dynamic_index_in_dim(real_form, half_index, 1, keepdims=False).reshape(
        gate_size, 2 * gate_size
    )
    flattened = amp_flat.reshape(2 * gate_size, amp_count // gate_size)
    result = jnp.dot(chosen, flattened, precision=HIGHEST, preferred_element_type=jnp.float32)
    return result.reshape(2, amp_count // 2)


def run_segment(amp_flat, seg_mats, gate_total):
    for number in range(gate_total):
        amp_flat = apply_gate(amp_flat, seg_mats[number], GATE_KINDS[number])
    return amp_flat


def join_halves(kept_half, received, own_bit, axis_pos):
    low_half = jnp.where(own_bit == 0, kept_half, received)
    high_half = jnp.where(own_bit == 0, received, kept_half)
    return jnp.stack([low_half, high_half], axis=axis_pos)


def swap_section(amp_flat, seg_mats, own_bit, mover):
    gate_total = seg_mats.shape[0]
    amp_count = amp_flat.shape[-1]
    amp_flat = run_segment(amp_flat, seg_mats, gate_total - 1)
    send_half = top_half(amp_flat, seg_mats[gate_total - 1], 1 - own_bit)
    received = mover(send_half)
    kept_half = top_half(amp_flat, seg_mats[gate_total - 1], own_bit)
    return join_halves(kept_half, received, own_bit, 1).reshape(2, amp_count)


def body(amplitudes, gate_matrices, permutation):
    amp_count = amplitudes.shape[-1]
    gate_total = gate_matrices.shape[1]
    amp_flat = amplitudes.reshape(2, amp_count)
    row_count = lax.axis_size("row")
    row_bits = row_count.bit_length() - 1
    col_bits = lax.axis_size("col").bit_length() - 1
    row_index = lax.axis_index("row")
    col_index = lax.axis_index("col")
    near_bit = row_index & 1
    amp_flat = swap_section(
        amp_flat, gate_matrices[0], near_bit, lambda outgoing: partner(outgoing, "row", 0)
    )
    far_bit = row_index >> row_bits - 1 & 1
    amp_flat = swap_section(
        amp_flat, gate_matrices[1], far_bit, lambda outgoing: partner(outgoing, "row", row_bits - 1)
    )
    amp_flat = run_segment(amp_flat, gate_matrices[2], gate_total)
    layout = amp_flat.reshape(2, row_count, amp_count // row_count)
    layout = lax.all_to_all(layout, "row", split_axis=1, concat_axis=1, tiled=True)
    layout = jnp.take(layout, permutation, axis=1)
    amp_flat = layout.reshape(2, amp_count)
    col_bit = col_index >> col_bits - 1 & 1
    amp_flat = swap_section(
        amp_flat, gate_matrices[3], col_bit, lambda outgoing: partner(outgoing, "col", col_bits - 1)
    )
    amp_flat = run_segment(amp_flat, gate_matrices[4], gate_total)
    return amp_flat.reshape(amplitudes.shape)


def solution(mesh):
    placed = (P(None, "row", "col", None), P(), P())
    return jax.shard_map(
        body, mesh=mesh, in_specs=placed, out_specs=P(None, "row", "col", None), check_vma=False
    )
```

profile of v0, /device:TPU:14, one launch (start us, length us, event | category | flops | bytes accessed | tf_op | source)
XLA Modules:
  0.0 295.0 jit_solution(1753980410946098717)
XLA Ops:
  0.0 2.3 fusion.103
  2.3 2.3 slice_bitcast_fusion.38
  4.6 2.4 slice_bitcast_fusion.39
  7.2 7.7 %reduce = f32[2,262144]{1,0:T(2,128)} reduce(f32[2,1,1,262144]{3,2,1,0:T(1,128)S(1)} %copy-done, f32[]{:T(128)} %constant.48), dimensions={1,2}, to_apply=%param.3.reduce_sub_computation | reduce | bytes 4194308 | tf_op args[0]
  14.9 3.4 %reshape_reshape.67 = f32[256,2048]{1,0:T(8,128)S(1)} reshape(f32[2,262144]{1,0:T(2,128)} %reduce) | data formatting | bytes 4194304 | tf_op jit(solution)/shard_map/reshape;reshape | solution.py:29
  18.3 3.2 %fusion.73 = f32[256,2048]{1,0:T(8,128)} fusion(f32[256,2048]{1,0:T(8,128)S(1)} %reshape_reshape.67, f32[128,128]{1,0:T(8,128)S(1)} %get-tuple-element.45, f32[128,128]{1,0:T(8,128)S(1)} %get-tuple-element.44, f32[128,128]{1,0:T(8,128)S(1)} %get-tuple-element.16), kind=kOutput, calls=%fused_computation.82 | convolution fusion | flops 1610809344 | bytes 4390912 | tf_op jit(solution)/shard_map/dot_general | solution.py:30
  23.3 2.0 fusion.10
  26.4 3.2 %convolution_bitcast_fusion.4 = f32[2,2048,128]{2,1,0:T(8,128)} fusion(f32[2,2048,128,1]{2,1,0,3:T(8,128)S(1)} %bitcast.261, f32[2,128,2,128]{3,2,1,0:T(2,128)S(1)} %reshape.220), kind=kOutput, calls=%fused_computation.5 | convolution fusion | flops 1610612736 | bytes 4456448 | tf_op jit(solution)/shard_map/djck,cmk->dmj/dot_general | solution.py:40
  29.5 13.6 %reshape_reshape.70 = f32[256,2048]{1,0:T(8,128)S(1)} reshape(f32[2,2048,128]{2,1,0:T(8,128)} %convolution_bitcast_fusion.4) | data formatting | bytes 4194304 | tf_op jit(solution)/shard_map/reshape;reshape | solution.py:50
  44.4 1.9 reshape.223
  50.5 1.9 select_bitcast_fusion.3
  54.2 3.2 %pad_maximum_fusion = f32[2,2,131072]{2,1,0:T(2,128)} fusion(f32[2,1,131072]{2,1,0:T(1,128)S(1)} %stack.28, f32[2,1,131072]{2,1,0:T(1,128)S(1)} %copy.39), kind=kLoop, calls=%fused_computation.6 | loop fusion | flops 524288 | bytes 4194304 | tf_op jit(solution)/shard_map/stack | solution.py:64
  57.4 3.1 %reshape_reshape.71 = f32[256,2048]{1,0:T(8,128)S(1)} reshape(f32[2,2,131072]{2,1,0:T(2,128)} %pad_maximum_fusion) | data formatting | bytes 4194304 | tf_op jit(solution)/shard_map/reshape;reshape | solution.py:29
  60.6 3.2 %fusion.65 = f32[256,2048]{1,0:T(8,128)} fusion(f32[256,2048]{1,0:T(8,128)S(1)} %reshape_reshape.71, f32[128,128]{1,0:T(8,128)S(1)} %copy-done.22, f32[128,128]{1,0:T(8,128)S(1)} %copy-done.21, f32[128,128]{1,0:T(8,128)S(1)} %copy-done.20), kind=kOutput, calls=%fused_computation.73 | convolution fusion | flops 1610809344 | bytes 4390912 | tf_op jit(solution)/shard_map/dot_general | solution.py:30
  65.5 2.0 fusion.13
  67.7 3.2 %convolution_bitcast_fusion.3 = f32[2,2048,128]{2,1,0:T(8,128)} fusion(f32[2,2048,128,1]{2,1,0,3:T(8,128)S(1)} %bitcast.262, f32[2,128,2,128]{3,2,1,0:T(2,128)S(1)} %reshape.225), kind=kOutput, calls=%fused_computation.4 | convolution fusion | flops 1610612736 | bytes 4456448 | tf_op jit(solution)/shard_map/djck,cmk->dmj/dot_general | solution.py:40
  70.9 2.1 reshape_reshape.74
  73.0 2.1 fusion.126
  75.2 1.9 reshape.228
  77.0 2.6 collective-permute-start.1
  86.2 39.2 %collective-permute-done.1 = f32[2,131072]{1,0:T(2,128)} collective-permute-done((f32[2,131072]{1,0:T(2,128)}, f32[2,131072]{1,0:T(2,128)}, u32[]{:S(2)}, u32[]{:S(2)}) %collective-permute-start.1) | collective-permute-done | bytes 1048608 | tf_op jit(solution)/shard_map/ppermute | solution.py:13
  125.4 1.9 select_bitcast_fusion.2
  129.2 3.2 %pad_maximum_fusion.1 = f32[2,2,131072]{2,1,0:T(2,128)} fusion(f32[2,1,131072]{2,1,0:T(1,128)S(1)} %stack.31, f32[2,1,131072]{2,1,0:T(1,128)S(1)} %copy.44), kind=kLoop, calls=%fused_computation.7 | loop fusion | flops 524288 | bytes 4194304 | tf_op jit(solution)/shard_map/stack | solution.py:64
  132.4 3.3 %reshape_reshape.75 = f32[256,2048]{1,0:T(8,128)S(1)} reshape(f32[2,2,131072]{2,1,0:T(2,128)} %pad_maximum_fusion.1) | data formatting | bytes 4194304 | tf_op jit(solution)/shard_map/reshape;reshape | solution.py:29
  135.7 3.2 %fusion.57 = f32[256,2048]{1,0:T(8,128)} fusion(f32[256,2048]{1,0:T(8,128)S(1)} %reshape_reshape.75, f32[128,128]{1,0:T(8,128)S(1)} %copy-done.19, f32[128,128]{1,0:T(8,128)S(1)} %copy-done.18, f32[128,128]{1,0:T(8,128)S(1)} %copy-done.15), kind=kOutput, calls=%fused_computation.64 | convolution fusion | flops 1610809344 | bytes 4390912 | tf_op jit(solution)/shard_map/dot_general | solution.py:30
  140.6 2.0 fusion.16
  143.6 3.2 %convolution_bitcast_fusion.2 = f32[2,2048,128]{2,1,0:T(8,128)} fusion(f32[2,2048,128,1]{2,1,0,3:T(8,128)S(1)} %bitcast.263, f32[2,128,2,128]{3,2,1,0:T(2,128)S(1)} %copy-done.5), kind=kOutput, calls=%fused_computation.3 | convolution fusion | flops 1610612736 | bytes 4456448 | tf_op jit(solution)/shard_map/djck,cmk->dmj/dot_general | solution.py:40
  148.6 3.2 %fusion.49 = f32[256,2048]{1,0:T(8,128)} fusion(f32[256,2048]{1,0:T(8,128)S(1)} %reshape_reshape.78, f32[128,128]{1,0:T(8,128)S(1)} %copy-done.17, f32[128,128]{1,0:T(8,128)S(1)} %copy-done.16, f32[128,128]{1,0:T(8,128)S(1)} %copy-done.14), kind=kOutput, calls=%fused_computation.56 | convolution fusion | flops 1610809344 | bytes 4390912 | tf_op jit(solution)/shard_map/dot_general | solution.py:30
  153.5 2.9 copy.49
  156.5 7.5 %all-to-all-start = ((f32[2,16,16384]{2,0,1:T(2,128)}), f32[2,16,16384]{2,0,1:T(2,128)S(1)}, u32[]{:S(2)}, u32[]{:S(2)}) async-start(f32[2,16,16384]{2,0,1:T(2,128)} %copy.49), calls=%async_computation | async-start | bytes 4194304 | tf_op jit(solution)/shard_map/all_to_all | solution.py:96
  165.9 45.3 %all-to-all-done = f32[2,16,16384]{2,0,1:T(2,128)S(1)} async-done(((f32[2,16,16384]{2,0,1:T(2,128)}), f32[2,16,16384]{2,0,1:T(2,128)S(1)}, u32[]{:S(2)}, u32[]{:S(2)}) %all-to-all-start) | async-done | bytes 2097184 | tf_op jit(solution)/shard_map/all_to_all | solution.py:96
  211.2 4.0 %gather_fusion = f32[16,2,16384]{2,1,0:T(2,128)} fusion(f32[2,16,16384]{2,0,1:T(2,128)S(1)} %all-to-all-done, s32[1024]{0:T(1024)S(1)} %pad_clamp_fusion), kind=kCustom, calls=%fused_computation | custom fusion | bytes 4194368 | tf_op jit(solution)/shard_map/jit(_take)/gather | solution.py:97
  215.2 2.7 select_bitcast_fusion
  217.9 2.5 copy.50
  222.2 3.2 %fusion.41 = f32[256,2048]{1,0:T(8,128)} fusion(f32[256,2048]{1,0:T(8,128)S(1)} %select_n.78, f32[128,128]{1,0:T(8,128)S(1)} %copy-done.13, f32[128,128]{1,0:T(8,128)S(1)} %copy-done.12, f32[128,128]{1,0:T(8,128)S(1)} %copy-done.11), kind=kOutput, calls=%fused_computation.48 | convolution fusion | flops 1610809344 | bytes 4390912 | tf_op jit(solution)/shard_map/dot_general | solution.py:30
  227.2 2.0 fusion.19
  229.4 3.2 %convolution_bitcast_fusion.1 = f32[2,2048,128]{2,1,0:T(8,128)} fusion(f32[2,2048,128,1]{2,1,0,3:T(8,128)S(1)} %bitcast.264, f32[2,128,2,128]{3,2,1,0:T(2,128)S(1)} %reshape.232), kind=kOutput, calls=%fused_computation.2 | convolution fusion | flops 1610612736 | bytes 4456448 | tf_op jit(solution)/shard_map/djck,cmk->dmj/dot_general | solution.py:40
  232.6 2.1 reshape_reshape.82
  234.7 2.2 fusion.128
  245.6 18.8 %collective-permute-done.2 = f32[2,131072]{1,0:T(2,128)} collective-permute-done((f32[2,131072]{1,0:T(2,128)}, f32[2,131072]{1,0:T(2,128)}, u32[]{:S(2)}, u32[]{:S(2)}) %collective-permute-start.2) | collective-permute-done | bytes 1048608 | tf_op jit(solution)/shard_map/ppermute | solution.py:13
  264.4 1.9 select_bitcast_fusion.1
  268.2 3.2 %pad_maximum_fusion.2 = f32[2,2,131072]{2,1,0:T(2,128)} fusion(f32[2,1,131072]{2,1,0:T(1,128)S(1)} %stack.34, f32[2,1,131072]{2,1,0:T(1,128)S(1)} %copy.55), kind=kLoop, calls=%fused_computation.8 | loop fusion | flops 524288 | bytes 4194304 | tf_op jit(solution)/shard_map/stack | solution.py:64
  271.4 3.3 %reshape_reshape.83 = f32[256,2048]{1,0:T(8,128)S(1)} reshape(f32[2,2,131072]{2,1,0:T(2,128)} %pad_maximum_fusion.2) | data formatting | bytes 4194304 | tf_op jit(solution)/shard_map/reshape;reshape | solution.py:29
  274.7 3.2 %fusion.33 = f32[256,2048]{1,0:T(8,128)} fusion(f32[256,2048]{1,0:T(8,128)S(1)} %reshape_reshape.83, f32[128,128]{1,0:T(8,128)S(1)} %copy-done.10, f32[128,128]{1,0:T(8,128)S(1)} %copy-done.9, f32[128,128]{1,0:T(8,128)S(1)} %copy-done.23), kind=kOutput, calls=%fused_computation.39 | convolution fusion | flops 1610809344 | bytes 4390912 | tf_op jit(solution)/shard_map/dot_general | solution.py:30
  279.7 2.0 fusion.22
  282.0 3.2 %convolution_bitcast_fusion = f32[2,2048,128]{2,1,0:T(8,128)} fusion(f32[2,2048,128,1]{2,1,0,3:T(8,128)S(1)} %bitcast.265, f32[2,128,2,128]{3,2,1,0:T(2,128)S(1)} %reshape.237), kind=kOutput, calls=%fused_computation.1 | convolution fusion | flops 1610612736 | bytes 4456448 | tf_op jit(solution)/shard_map/djck,cmk->dmj/dot_general | solution.py:40
  286.9 3.2 %fusion.25 = f32[256,2048]{1,0:T(8,128)} fusion(f32[256,2048]{1,0:T(8,128)S(1)} %reshape_reshape.86, f32[128,128]{1,0:T(8,128)S(1)} %copy-done.8, f32[128,128]{1,0:T(8,128)S(1)} %copy-done.7, f32[128,128]{1,0:T(8,128)S(1)} %copy-done.6), kind=kOutput, calls=%fused_computation.31 | convolution fusion | flops 1610809344 | bytes 4390912 | tf_op jit(solution)/shard_map/dot_general | solution.py:30
  290.1 4.7 %reshape_reshape.88 = f32[2,1,1,262144]{3,2,1,0:T(1,128)} reshape(f32[256,2048]{1,0:T(8,128)} %fusion.25) | data formatting | bytes 4194304 | tf_op jit(solution)/shard_map/reshape;reshape | solution.py:104
  (148 shorter events, 46.3 us)
Async XLA Ops:
  4.6 2.6 copy-start
  25.3 0.9 copy-start.44
  46.3 4.2 %collective-permute-start = (f32[2,131072]{1,0:T(2,128)}, f32[2,131072]{1,0:T(2,128)}, u32[]{:S(2)}, u32[]{:S(2)}) collective-permute-start(f32[2,131072]{1,0:T(2,128)} %reshape.223), channel_id=1, source_target_pairs={{0,2},{2,0},{4,6},{6,4},{8,10},{10,8},{12,14},{14,12},{16,18},{18,... | collective-permute-start | bytes 3145736 | tf_op jit(solution)/shard_map/ppermute | solution.py:13
  47.5 1.2 copy-start.32
  47.5 1.2 copy-start.33
  47.5 1.2 copy-start.38
  47.6 1.2 copy-start.39
  47.6 1.2 copy-start.40
  47.6 1.2 copy-start.41
  47.6 2.1 copy-start.30
  47.6 2.1 copy-start.31
  47.6 2.1 copy-start.34
  47.6 2.1 copy-start.35
  47.6 2.1 copy-start.36
  47.6 2.1 copy-start.37
  57.4 3.1 %copy-start.20 = (f32[128,128]{1,0:T(8,128)S(1)}, f32[128,128]{1,0:T(8,128)}, u32[]{:S(2)}) copy-start(f32[128,128]{1,0:T(8,128)} %get-tuple-element.18) | copy-start | bytes 196612
  57.4 3.1 %copy-start.21 = (f32[128,128]{1,0:T(8,128)S(1)}, f32[128,128]{1,0:T(8,128)}, u32[]{:S(2)}) copy-start(f32[128,128]{1,0:T(8,128)} %get-tuple-element.48) | copy-start | bytes 196612
  57.4 3.1 %copy-start.22 = (f32[128,128]{1,0:T(8,128)S(1)}, f32[128,128]{1,0:T(8,128)}, u32[]{:S(2)}) copy-start(f32[128,128]{1,0:T(8,128)} %get-tuple-element.49) | copy-start | bytes 196612
  77.0 48.4 %collective-permute-start.1 = (f32[2,131072]{1,0:T(2,128)}, f32[2,131072]{1,0:T(2,128)}, u32[]{:S(2)}, u32[]{:S(2)}) collective-permute-start(f32[2,131072]{1,0:T(2,128)} %reshape.228), channel_id=1, source_target_pairs={{0,16},{2,18},{4,20},{6,22},{8,24},{10,26},{12,28},{14,30},{16,0},... | collective-permute-start | bytes 3145736 | tf_op jit(solution)/shard_map/ppermute | solution.py:13
  132.4 3.3 %copy-start.15 = (f32[128,128]{1,0:T(8,128)S(1)}, f32[128,128]{1,0:T(8,128)}, u32[]{:S(2)}) copy-start(f32[128,128]{1,0:T(8,128)} %get-tuple-element.20) | copy-start | bytes 196612
  132.4 3.3 %copy-start.18 = (f32[128,128]{1,0:T(8,128)S(1)}, f32[128,128]{1,0:T(8,128)}, u32[]{:S(2)}) copy-start(f32[128,128]{1,0:T(8,128)} %get-tuple-element.52) | copy-start | bytes 196612
  132.4 3.3 %copy-start.19 = (f32[128,128]{1,0:T(8,128)S(1)}, f32[128,128]{1,0:T(8,128)}, u32[]{:S(2)}) copy-start(f32[128,128]{1,0:T(8,128)} %get-tuple-element.53) | copy-start | bytes 196612
  138.9 1.8 copy-start.3
  142.7 1.0 copy-start.5
  146.8 1.8 copy-start.14
  146.8 1.8 copy-start.16
  146.8 1.8 copy-start.17
  156.5 7.5 %copy-start.1 = (f32[256,256]{1,0:T(8,128)S(1)}, f32[256,256]{1,0:T(8,128)}, u32[]{:S(2)}) copy-start(f32[256,256]{1,0:T(8,128)} %get-tuple-element.85) | copy-start | bytes 786436
  156.5 7.7 %copy-start.24 = (f32[128,128]{1,0:T(8,128)S(1)}, f32[128,128]{1,0:T(8,128)}, u32[]{:S(2)}) copy-start(f32[128,128]{1,0:T(8,128)} %get-tuple-element.7) | copy-start | bytes 196612
  156.5 7.7 %copy-start.25 = (f32[128,128]{1,0:T(8,128)S(1)}, f32[128,128]{1,0:T(8,128)}, u32[]{:S(2)}) copy-start(f32[128,128]{1,0:T(8,128)} %get-tuple-element.8) | copy-start | bytes 196612
  156.5 7.7 %copy-start.26 = (f32[128,128]{1,0:T(8,128)S(1)}, f32[128,128]{1,0:T(8,128)}, u32[]{:S(2)}) copy-start(f32[128,128]{1,0:T(8,128)} %get-tuple-element.25) | copy-start | bytes 196612
  156.5 7.7 %copy-start.27 = (f32[128,128]{1,0:T(8,128)S(1)}, f32[128,128]{1,0:T(8,128)}, u32[]{:S(2)}) copy-start(f32[128,128]{1,0:T(8,128)} %get-tuple-element.26) | copy-start | bytes 196612
  156.5 7.7 %copy-start.28 = (f32[128,128]{1,0:T(8,128)S(1)}, f32[128,128]{1,0:T(8,128)}, u32[]{:S(2)}) copy-start(f32[128,128]{1,0:T(8,128)} %get-tuple-element.27) | copy-start | bytes 196612
  156.5 7.7 %copy-start.29 = (f32[128,128]{1,0:T(8,128)S(1)}, f32[128,128]{1,0:T(8,128)}, u32[]{:S(2)}) copy-start(f32[128,128]{1,0:T(8,128)} %get-tuple-element.28) | copy-start | bytes 196612
  156.5 8.6 %copy-start.45 = (s32[16]{0:T(128)S(1)}, s32[16]{0:T(128)}, u32[]{:S(2)}) copy-start(s32[16]{0:T(128)} %param.5) | copy-start | bytes 196
  156.5 54.6 %all-to-all-start = ((f32[2,16,16384]{2,0,1:T(2,128)}), f32[2,16,16384]{2,0,1:T(2,128)S(1)}, u32[]{:S(2)}, u32[]{:S(2)}) async-start(f32[2,16,16384]{2,0,1:T(2,128)} %copy.49), calls=%async_computation | async-start | bytes 4194304 | tf_op jit(solution)/shard_map/all_to_all | solution.py:96
  220.4 1.8 copy-start.11
  220.4 1.8 copy-start.12
  220.4 1.8 copy-start.13
  234.7 4.6 %copy-start.2 = (f32[256,256]{1,0:T(8,128)S(1)}, f32[256,256]{1,0:T(8,128)}, u32[]{:S(2)}) copy-start(f32[256,256]{1,0:T(8,128)} %get-tuple-element.87) | copy-start | bytes 786436
  238.8 25.7 %collective-permute-start.2 = (f32[2,131072]{1,0:T(2,128)}, f32[2,131072]{1,0:T(2,128)}, u32[]{:S(2)}, u32[]{:S(2)}) collective-permute-start(f32[2,131072]{1,0:T(2,128)} %reshape.235), channel_id=1, source_target_pairs={{0,1},{1,0},{2,3},{3,2},{4,5},{5,4},{6,7},{7,6},{8,9},{9,8},{10,11... | collective-permute-start | bytes 3145736 | tf_op jit(solution)/shard_map/ppermute | solution.py:13
  271.4 3.3 %copy-start.9 = (f32[128,128]{1,0:T(8,128)S(1)}, f32[128,128]{1,0:T(8,128)}, u32[]{:S(2)}) copy-start(f32[128,128]{1,0:T(8,128)} %get-tuple-element.60) | copy-start | bytes 196612
  271.4 3.3 %copy-start.10 = (f32[128,128]{1,0:T(8,128)S(1)}, f32[128,128]{1,0:T(8,128)}, u32[]{:S(2)}) copy-start(f32[128,128]{1,0:T(8,128)} %get-tuple-element.61) | copy-start | bytes 196612
  271.4 3.3 %copy-start.23 = (f32[128,128]{1,0:T(8,128)S(1)}, f32[128,128]{1,0:T(8,128)}, u32[]{:S(2)}) copy-start(f32[128,128]{1,0:T(8,128)} %fusion.104) | copy-start | bytes 196612
  277.9 1.8 copy-start.4
  285.1 1.8 copy-start.6
  285.1 1.8 copy-start.7
  285.1 1.8 copy-start.8
  (2 other events, 1.7 us)
where the time goes:
time: 299 us; the launch traced here: 295 us
  waiting for transfers between devices  103 us (34%)
  local copies, waits for them, and re-layouts  88.4 us (30%)
  matrix products  57.6 us (19%)
  other arithmetic  34 us (11%)
  starting transfers between devices  10.6 us (4%)
    ppermute x3, waiting for transfers between devices, partner(): return lax.ppermute(value, axis, pairs)  58 us
    all_to_all x1, waiting for transfers between devices, body(): lax.all_to_all(layout, 'row', split_axis=1, concat_axis=1, tiled=True)  45.3 us
    dot_general x7, matrix products, apply_gate(): jnp.dot(real_form, flattened, precision=HIGHEST, preferred_element_type=j...  22.4 us
    another operation x3, local copies, waits for them, and re-layouts, top_half(): flattened = amp_flat.reshape(2 * gate_size, amp_count // gate_size)  17.8 us
    another operation x6, local copies, waits for them, and re-layouts, apply_gate(): flattened = amp_flat.reshape(2 * gate_size, amp_count // gate_size)  16.5 us
    dot_general x5, matrix products, apply_gate(): jnp.einsum('djck,cmk->dmj', real_quad, columns, precision=HIGHEST)  15.8 us
    another operation x6, other arithmetic, join_halves(): return jnp.stack([low_half, high_half], axis=axis_pos)  15.5 us
    dot_general x5, matrix products, apply_gate(): jnp.einsum('djck,cakb->dajb', real_quad, blocks, precision=HIGHEST)  10.1 us
  transfers between devices with their start and end apart: 4, of which 3 were waited for; matrix products, arithmetic and copies ran while one was open for 6% of the time, Pallas kernels for 0%

commit v1 on v0

v1 whole, which is shorter than its diff:
```python
import functools

import jax
import jax.numpy as jnp
from jax import lax
from jax.experimental import pallas as pl
from jax.experimental.pallas import tpu as pltpu
from jax.sharding import PartitionSpec as P

HIGHEST = lax.Precision.HIGHEST
MESH = pl.DeviceIdType.MESH
F32 = jnp.float32
BF16 = jnp.bfloat16


def split(value):
    high = value.astype(BF16)
    return high, (value - high.astype(F32)).astype(BF16)


def dot32(left, right):
    return jnp.dot(left, right, preferred_element_type=F32)


def product(left, right):
    left_high, left_low = split(left)
    right_high, right_low = split(right)
    return (
        dot32(left_high, right_high)
        + dot32(left_high, right_low)
        + dot32(left_low, right_high)
    )


def real_form(real_part, imag_part):
    return jnp.concatenate(
        [
            jnp.concatenate([real_part, -imag_part], axis=1),
            jnp.concatenate([imag_part, real_part], axis=1),
        ],
        axis=0,
    )


def real_form_transposed(real_part, imag_part):
    real_t, imag_t = real_part.T, imag_part.T
    return jnp.concatenate(
        [
            jnp.concatenate([real_t, imag_t], axis=1),
            jnp.concatenate([-imag_t, real_t], axis=1),
        ],
        axis=0,
    )


def kernel(
    rows,
    cols,
    amp_ref,
    gates_ref,
    mids_ref,
    first_ref,
    out_ref,
    state,
    weight,
    low_weight,
    arrived,
    stage,
    blocks,
    swap_send,
    swap_recv,
    map_send,
    map_recv,
):
    kk, _, high, low, lanes = state.shape
    order = high * low
    chunks = kk // 2
    rest = order // rows
    half = high // 2
    r = lax.axis_index("row")
    c = lax.axis_index("col")

    barrier = pltpu.get_barrier_semaphore()
    near = r + 1 - 2 * (r % 2)
    far_bit = r // (rows // 2)
    far = r + rows // 2 - rows * far_bit
    col_bit = c // (cols // 2)
    across = c + cols // 2 - cols * col_bit
    for step in range(1, rows):
        pl.semaphore_signal(
            barrier, inc=1, device_id=((r + step) % rows, c), device_id_type=MESH
        )
    pl.semaphore_signal(barrier, inc=1, device_id=(r, across), device_id_type=MESH)

    def set_weight(real_part, imag_part):
        top, bottom = split(real_form(real_part, imag_part))
        size = 2 * order
        weight[:, 0:size] = top
        weight[:, size : 2 * size] = top
        weight[:, 2 * size : 3 * size] = bottom

    def apply(value):
        top, bottom = split(value)
        return dot32(weight[...], jnp.concatenate([top, bottom, top], axis=0))

    def put(i, result):
        state[2 * i] = result[:, :lanes].reshape(2, high, low, lanes)
        state[2 * i + 1] = result[:, lanes:].reshape(2, high, low, lanes)

    def get(i):
        return jnp.concatenate(
            [
                state[2 * i].reshape(2 * order, lanes),
                state[2 * i + 1].reshape(2 * order, lanes),
            ],
            axis=1,
        )

    def top_step(i):
        put(i, apply(get(i)))

    def middle(seg):
        set_weight(mids_ref[seg, 0], mids_ref[seg, 1])

        def step(p, carry):
            def part(position):
                return jnp.concatenate(
                    [
                        state[:, 0, position].reshape(order, lanes),
                        state[:, 1, position].reshape(order, lanes),
                    ],
                    axis=0,
                )

            result = apply(jnp.concatenate([part(2 * p), part(2 * p + 1)], axis=1))
            for own in range(2):
                piece = result[:, own * lanes : (own + 1) * lanes]
                for d in range(2):
                    state[:, d, 2 * p + own] = piece[
                        d * order : (d + 1) * order
                    ].reshape(kk, low, lanes)
            return carry

        lax.fori_loop(0, high // 2, step, 0)

    def swap_copy(which, i, bit, device):
        return pltpu.make_async_remote_copy(
            src_ref=state.at[pl.ds(2 * i, 2), :, pl.ds((1 - bit) * half, half)],
            dst_ref=arrived.at[which, pl.ds(2 * i, 2)],
            send_sem=swap_send.at[which, i],
            recv_sem=swap_recv.at[which, i],
            device_id=device,
            device_id_type=MESH,
        )

    def lows(value):
        parts = jnp.concatenate([value[0], value[1]], axis=1)
        top, bottom = split(parts)
        joined = jnp.concatenate([top, bottom, top], axis=1)
        result = dot32(joined, low_weight[...])
        return jnp.stack([result[:, :lanes], result[:, lanes:]], axis=0)

    def swap_out(seg, which, bit, device):
        set_weight(gates_ref[seg, 3, 0], gates_ref[seg, 3, 1])

        def send(i, carry):
            top_step(i)
            swap_copy(which, i, bit, device).start()
            return carry

        lax.fori_loop(0, chunks, send, 0)

    def swap_in(seg, which, bit, device, with_lows):
        set_weight(gates_ref[seg, 0, 0], gates_ref[seg, 0, 1])

        def receive(i, carry):
            swap_copy(which, i, bit, device).wait()
            for own in range(2):
                piece = arrived[which, 2 * i + own]
                if with_lows:
                    piece = lows(piece.reshape(2, half * low, lanes)).reshape(
                        piece.shape
                    )
                state[2 * i + own, :, pl.ds((1 - bit) * half, half)] = piece
            top_step(i)
            return carry

        lax.fori_loop(0, chunks, receive, 0)

    set_weight(gates_ref[0, 0, 0], gates_ref[0, 0, 1])

    def load(i, carry):
        value = jnp.concatenate(
            [
                amp_ref[pl.ds(2 * i, 2 * order, stride=kk), :],
                amp_ref[pl.ds(2 * i + 1, 2 * order, stride=kk), :],
            ],
            axis=1,
        )
        put(i, apply(value))
        return carry

    lax.fori_loop(0, chunks, load, 0)
    middle(0)
    pl.semaphore_wait(barrier, rows)
    near_bit = r % 2
    swap_out(0, 0, near_bit, (near, c))
    swap_in(1, 0, near_bit, (near, c), False)
    middle(1)
    swap_out(1, 1, far_bit, (far, c))

    merged = real_form_transposed(gates_ref[0, 2, 0], gates_ref[0, 2, 1])
    for seg in range(1, gates_ref.shape[0]):
        merged = product(
            merged, real_form_transposed(gates_ref[seg, 2, 0], gates_ref[seg, 2, 1])
        )
    top, bottom = split(merged)
    low_weight[0 : 2 * lanes] = top
    low_weight[2 * lanes : 4 * lanes] = top
    low_weight[4 * lanes : 6 * lanes] = bottom

    def keep(i, carry):
        piece = state[i, :, pl.ds(far_bit * half, half)]
        state[i, :, pl.ds(far_bit * half, half)] = lows(
            piece.reshape(2, half * low, lanes)
        ).reshape(piece.shape)
        return carry

    lax.fori_loop(0, kk, keep, 0)
    swap_in(2, 1, far_bit, (far, c), True)
    middle(2)
    set_weight(gates_ref[2, 3, 0], gates_ref[2, 3, 1])

    def map_copy(i, step):
        target = (r + step) % rows
        return pltpu.make_async_remote_copy(
            src_ref=stage.at[i, target],
            dst_ref=blocks.at[i, r],
            send_sem=map_send.at[i, step],
            recv_sem=map_recv.at[i, step],
            device_id=(target, c),
            device_id_type=MESH,
        )

    def map_out(i, carry):
        result = apply(get(i))
        for own in range(2):
            for d in range(2):
                piece = result[
                    d * order : (d + 1) * order, own * lanes : (own + 1) * lanes
                ]
                if rest == 8:
                    stage[i, :, d, own * rest : (own + 1) * rest] = piece.reshape(
                        rows, rest, lanes
                    )
                else:
                    for t in range(rows):
                        stage[i, t, d, own * rest : (own + 1) * rest] = piece[
                            t * rest : (t + 1) * rest
                        ]
        for step in range(1, rows):
            map_copy(i, step).start()
        blocks[i, r] = stage[i, r]
        return carry

    lax.fori_loop(0, chunks, map_out, 0)
    set_weight(first_ref[0], first_ref[1])

    def map_in(i, carry):
        for step in range(1, rows):
            map_copy(i, step).wait()
        columns = []
        for own in range(2):
            if rest == 8:
                pieces = [
                    blocks[i, :, d, own * rest : (own + 1) * rest].reshape(order, lanes)
                    for d in range(2)
                ]
            else:
                pieces = [
                    blocks[i, s, d, own * rest : (own + 1) * rest]
                    for d in range(2)
                    for s in range(rows)
                ]
            columns.append(jnp.concatenate(pieces, axis=0))
        put(i, apply(jnp.concatenate(columns, axis=1)))
        return carry

    lax.fori_loop(0, chunks, map_in, 0)
    middle(3)
    swap_out(3, 2, col_bit, (r, across))
    swap_in(4, 2, col_bit, (r, across), False)
    middle(4)
    set_weight(gates_ref[4, 3, 0], gates_ref[4, 3, 1])

    def finish(i, carry):
        result = apply(get(i))
        out_ref[pl.ds(2 * i, 2 * order, stride=kk), :] = result[:, :lanes]
        out_ref[pl.ds(2 * i + 1, 2 * order, stride=kk), :] = result[:, lanes:]
        return carry

    lax.fori_loop(0, chunks, finish, 0)


def body(amplitudes, gate_matrices, permutation):
    rows = lax.axis_size("row")
    cols = lax.axis_size("col")
    segs = gate_matrices.shape[0]
    order = gate_matrices.shape[-1]
    amp_count = amplitudes.shape[-1]
    high = amp_count // (order * order)
    low = order // high
    kk = order // low
    rest = order // rows
    chunks = kk // 2
    mids = gate_matrices[:, 1].reshape(segs, 2, low, kk, low, kk)
    mids = mids.transpose(0, 1, 3, 2, 5, 4).reshape(segs, 2, order, order)
    chosen = (permutation[:, None] == jnp.arange(rows)[None, :]).astype(F32)
    first = jnp.einsum(
        "xjtw,ts->xjsw",
        gate_matrices[3, 0].reshape(2, order, rows, rest),
        chosen,
        precision=HIGHEST,
    ).reshape(2, order, order)
    vmem = pl.BlockSpec(memory_space=pltpu.VMEM)
    result = pl.pallas_call(
        functools.partial(kernel, rows, cols),
        out_shape=jax.ShapeDtypeStruct((2 * amp_count // order, order), F32),
        in_specs=[vmem] * 4,
        out_specs=vmem,
        scratch_shapes=[
            pltpu.VMEM((kk, 2, high, low, order), F32),
            pltpu.VMEM((2 * order, 6 * order), BF16),
            pltpu.VMEM((6 * order, 2 * order), BF16),
            pltpu.VMEM((3, kk, 2, high // 2, low, order), F32),
            pltpu.VMEM((chunks, rows, 2, 2 * rest, order), F32),
            pltpu.VMEM((chunks, rows, 2, 2 * rest, order), F32),
            pltpu.SemaphoreType.DMA((3, chunks)),
            pltpu.SemaphoreType.DMA((3, chunks)),
            pltpu.SemaphoreType.DMA((chunks, rows)),
            pltpu.SemaphoreType.DMA((chunks, rows)),
        ],
        compiler_params=pltpu.CompilerParams(
            collective_id=0, has_side_effects=True, vmem_limit_bytes=40 * 2**20
        ),
    )(amplitudes.reshape(2 * amp_count // order, order), gate_matrices, mids, first)
    return result.reshape(amplitudes.shape)


def solution(mesh):
    placed = (P(None, "row", "col", None), P(), P())
    return jax.shard_map(
        body, mesh=mesh, in_specs=placed, out_specs=P(None, "row", "col", None), check_vma=False
    )
```

time: 299 us -> 169 us (0.57)
  the two profiles are of different devices: /device:TPU:14 before, /device:TPU:0 now
where the time goes in v1:
time: 169 us
  Pallas kernels  145 us (86%)
  local copies, waits for them, and re-layouts  24 us (14%)
    pallas_call x1, Pallas kernels, body(): pl.pallas_call(functools.partial(kernel, rows, cols), out_shape=jax.Shape...  145 us
    another operation x2, local copies, waits for them, and re-layouts, body(): mids = gate_matrices[:, 1].reshape(segs, 2, low, kk, low, kk)  11.7 us
    reshape x1, local copies, waits for them, and re-layouts, body(): mids = mids.transpose(0, 1, 3, 2, 5, 4).reshape(segs, 2, order, order)  8.01 us

profile of v1, /device:TPU:0, one launch (start us, length us, event | category | flops | bytes accessed | tf_op | source)
XLA Modules:
  0.0 168.9 jit_solution(12464347897323608360)
XLA Ops:
  0.0 1.1 slice.6
  1.1 3.1 %reshape_squeeze.6 = f32[5,2,8,16,8,16]{5,4,3,2,1,0:T(8,128)} reshape(f32[5,1,2,128,128]{4,3,2,1,0:T(8,128)S(1)} %slice.6) | data formatting | bytes 1310720 | tf_op jit(solution)/shard_map/reshape;squeeze | solution.py:316
  4.3 8.6 %copy.7 = f32[5,2,8,16,8,16]{4,5,2,3,1,0:T(8,128)} copy(f32[5,2,8,16,8,16]{5,4,3,2,1,0:T(8,128)} %reshape_squeeze.6) | data formatting | bytes 1310720 | tf_op jit(solution)/shard_map/reshape;squeeze | solution.py:316
  12.8 0.0 copy-start
  12.8 0.0 copy-start.2
  12.8 8.0 %reshape.14.mids_ref = f32[5,2,128,128]{3,2,1,0:T(8,128)S(1)} reshape(f32[5,2,16,8,16,8]{5,4,3,2,1,0:T(8,128)} %bitcast.20) | data formatting | bytes 1310720 | tf_op jit(solution)/shard_map/reshape | solution.py:317
  20.9 0.0 copy-done
  20.9 0.1 copy.14
  21.0 0.0 copy-done.2
  21.0 0.2 convolution_bitcast_fusion
  21.3 0.1 copy.11.first_ref
  21.4 0.0 copy-start.1
  21.4 1.6 copy-done.1
  23.0 144.6 %shard_map.37 = f32[4096,128]{1,0:T(8,128)S(1)} custom-call(f32[4096,128]{1,0:T(8,128)S(1)} %bitcast.19, f32[5,4,2,128,128]{4,3,2,1,0:T(8,128)S(1)} %copy-done, f32[5,2,128,128]{3,2,1,0:T(8,128)S(1)} %reshape.14.mids_ref, f32[2,128,128]{2,1,0:T(8,128)S(1)} %copy.11.first_ref), custom_call_target="tpu_custom_call" | custom-call | tf_op jit(solution)/shard_map/pallas_call | solution.py:326
  167.6 1.3 copy.20
  (2 shorter events, 0.1 us)
Async XLA Ops:
  12.8 8.0 %copy-start = (f32[5,4,2,128,128]{4,3,2,1,0:T(8,128)S(1)}, f32[5,4,2,128,128]{4,3,2,1,0:T(8,128)}, u32[]{:S(2)}) copy-start(f32[5,4,2,128,128]{4,3,2,1,0:T(8,128)} %gates_ref.1) | copy-start | bytes 7864324
  12.8 8.2 %copy-start.2 = (s32[16]{0:T(128)S(1)}, s32[16]{0:T(128)}, u32[]{:S(2)}) copy-start(s32[16]{0:T(128)} %param.5) | copy-start | bytes 196
  21.4 1.6 copy-start.1

commit v2 on v1

--- a/solution.py
+++ b/solution.py
@@ -58,7 +58,6 @@
     cols,
     amp_ref,
     gates_ref,
-    mids_ref,
     first_ref,
     out_ref,
     state,
@@ -92,12 +91,19 @@
         )
     pl.semaphore_signal(barrier, inc=1, device_id=(r, across), device_id_type=MESH)
 
-    def set_weight(real_part, imag_part):
-        top, bottom = split(real_form(real_part, imag_part))
+    def place_weight(top, bottom):
         size = 2 * order
         weight[:, 0:size] = top
         weight[:, size : 2 * size] = top
         weight[:, 2 * size : 3 * size] = bottom
+
+    def set_weight(real_part, imag_part):
+        place_weight(*split(real_form(real_part, imag_part)))
+
+    def reorder_matrix():
+        new = lax.broadcasted_iota(jnp.int32, (order, order), 0)
+        old = lax.broadcasted_iota(jnp.int32, (order, order), 1)
+        return ((new % low) * kk + new // low == old).astype(F32).astype(BF16)
 
     def apply(value):
         top, bottom = split(value)
@@ -120,7 +126,19 @@
         put(i, apply(get(i)))
 
     def middle(seg):
-        set_weight(mids_ref[seg, 0], mids_ref[seg, 1])
+        reorder = reorder_matrix()
+
+        def moved(part):
+            rows_moved = dot32(reorder, part).astype(BF16)
+            return lax.dot_general(
+                rows_moved, reorder, (((1,), (1,)), ((), ())), preferred_element_type=F32
+            ).astype(BF16)
+
+        real_parts = split(gates_ref[seg, 1, 0])
+        imag_parts = split(gates_ref[seg, 1, 1])
+        place_weight(
+            *(real_form(moved(re), moved(im)) for re, im in zip(real_parts, imag_parts))
+        )
 
         def step(p, carry):
             def part(position):
@@ -305,7 +323,6 @@
 def body(amplitudes, gate_matrices, permutation):
     rows = lax.axis_size("row")
     cols = lax.axis_size("col")
-    segs = gate_matrices.shape[0]
     order = gate_matrices.shape[-1]
     amp_count = amplitudes.shape[-1]
     high = amp_count // (order * order)
@@ -313,8 +330,6 @@
     kk = order // low
     rest = order // rows
     chunks = kk // 2
-    mids = gate_matrices[:, 1].reshape(segs, 2, low, kk, low, kk)
-    mids = mids.transpose(0, 1, 3, 2, 5, 4).reshape(segs, 2, order, order)
     chosen = (permutation[:, None] == jnp.arange(rows)[None, :]).astype(F32)
     first = jnp.einsum(
         "xjtw,ts->xjsw",
@@ -326,7 +341,7 @@
     result = pl.pallas_call(
         functools.partial(kernel, rows, cols),
         out_shape=jax.ShapeDtypeStruct((2 * amp_count // order, order), F32),
-        in_specs=[vmem] * 4,
+        in_specs=[vmem] * 3,
         out_specs=vmem,
         scratch_shapes=[
             pltpu.VMEM((kk, 2, high, low, order), F32),
@@ -343,7 +358,7 @@
         compiler_params=pltpu.CompilerParams(
             collective_id=0, has_side_effects=True, vmem_limit_bytes=40 * 2**20
         ),
-    )(amplitudes.reshape(2 * amp_count // order, order), gate_matrices, mids, first)
+    )(amplitudes.reshape(2 * amp_count // order, order), gate_matrices, first)
     return result.reshape(amplitudes.shape)
 
 

time: 169 us -> 153 us (0.905)
  local copies, waits for them, and re-layouts: 24 us -> 5.79 us
  Pallas kernels: 145 us -> 147 us
    another operation x2 -> x0, local copies, waits for them, and re-layouts: 11.7 us -> none  [body(): mids = gate_matrices[:, 1].reshape(segs, 2, low, kk, low, kk)]
    reshape x1 -> x0, local copies, waits for them, and re-layouts: 8.01 us -> none  [body(): mids = mids.transpose(0, 1, 3, 2, 5, 4).reshape(segs, 2, order, order)]
    pallas_call x1, Pallas kernels: 145 us -> 147 us  [body(): pl.pallas_call(functools.partial(kernel, rows, cols), out_shape=jax.Shape...]
    unnamed x8 -> x6, local copies, waits for them, and re-layouts: 3.01 us -> 4.74 us
where the time goes in v2:
time: 153 us
  Pallas kernels  147 us (96%)
  local copies, waits for them, and re-layouts  5.79 us (4%)
    pallas_call x1, Pallas kernels, body(): pl.pallas_call(functools.partial(kernel, rows, cols), out_shape=jax.Shape...  147 us
    unnamed x6, local copies, waits for them, and re-layouts  4.74 us

profile of v2, /device:TPU:0, one launch (start us, length us, event | category | flops | bytes accessed | tf_op | source)
XLA Modules:
  0.0 153.2 jit_solution(963369227847274171)
XLA Ops:
  0.0 0.9 slice.3
  0.9 0.1 copy.12
  1.0 0.9 convolution_bitcast_fusion
  1.9 0.1 copy.9.first_ref
  2.0 0.0 copy-start
  2.1 1.7 %copy-done = f32[5,4,2,128,128]{4,3,2,1,0:T(8,128)S(1)} copy-done((f32[5,4,2,128,128]{4,3,2,1,0:T(8,128)S(1)}, f32[5,4,2,128,128]{4,3,2,1,0:T(8,128)}, u32[]{:S(2)}) %copy-start) | copy-done | bytes 2621464
  3.8 0.0 copy-start.1
  3.8 1.6 %copy-done.1 = f32[2,1,1,262144]{3,2,1,0:T(1,128)S(1)} copy-done((f32[2,1,1,262144]{3,2,1,0:T(1,128)S(1)}, f32[2,1,1,262144]{3,2,1,0:T(1,128)}, u32[]{:S(2)}) %copy-start.1) | copy-done | bytes 2097176
  5.4 146.5 %shard_map.37 = f32[4096,128]{1,0:T(8,128)S(1)} custom-call(f32[4096,128]{1,0:T(8,128)S(1)} %bitcast.14, f32[5,4,2,128,128]{4,3,2,1,0:T(8,128)S(1)} %copy-done, f32[2,128,128]{2,1,0:T(8,128)S(1)} %copy.9.first_ref), custom_call_target="tpu_custom_call" | custom-call | tf_op jit(solution)/shard_map/pallas_call | solution.py:341
  151.9 1.3 copy.18
  (1 shorter events, 0.0 us)
Async XLA Ops:
  2.0 1.7 %copy-start = (f32[5,4,2,128,128]{4,3,2,1,0:T(8,128)S(1)}, f32[5,4,2,128,128]{4,3,2,1,0:T(8,128)}, u32[]{:S(2)}) copy-start(f32[5,4,2,128,128]{4,3,2,1,0:T(8,128)} %gates_ref.1) | copy-start | bytes 7864324
  3.8 1.6 %copy-start.1 = (f32[2,1,1,262144]{3,2,1,0:T(1,128)S(1)}, f32[2,1,1,262144]{3,2,1,0:T(1,128)}, u32[]{:S(2)}) copy-start(f32[2,1,1,262144]{3,2,1,0:T(1,128)} %param.3) | copy-start | bytes 6291460

commit v3 on v1

v3 whole, which is shorter than its diff:
```python
import functools

import jax
import jax.numpy as jnp
from jax import lax
from jax.experimental import pallas as pl
from jax.experimental.pallas import tpu as pltpu
from jax.sharding import PartitionSpec as P

HIGHEST = lax.Precision.HIGHEST
MESH = pl.DeviceIdType.MESH
F32 = jnp.float32
BF16 = jnp.bfloat16


def split(value):
    high = value.astype(BF16)
    return high, (value - high.astype(F32)).astype(BF16)


def dot32(left, right):
    return jnp.dot(left, right, preferred_element_type=F32)


def product(left, right):
    left_high, left_low = split(left)
    right_high, right_low = split(right)
    return (
        dot32(left_high, right_high)
        + dot32(left_high, right_low)
        + dot32(left_low, right_high)
    )


def real_form(real_part, imag_part):
    return jnp.concatenate(
        [
            jnp.concatenate([real_part, -imag_part], axis=1),
            jnp.concatenate([imag_part, real_part], axis=1),
        ],
        axis=0,
    )


def real_form_transposed(real_part, imag_part):
    real_t, imag_t = real_part.T, imag_part.T
    return jnp.concatenate(
        [
            jnp.concatenate([real_t, imag_t], axis=1),
            jnp.concatenate([-imag_t, real_t], axis=1),
        ],
        axis=0,
    )


def kernel(
    rows,
    cols,
    amp_ref,
    gates_ref,
    first_ref,
    out_ref,
    state,
    weight,
    low_weight,
    arrived,
    stage,
    blocks,
    swap_send,
    swap_recv,
    map_send,
    map_recv,
):
    kk, _, high, low, lanes = state.shape
    order = high * low
    chunks = kk // 2
    rest = order // rows
    half = high // 2
    r = lax.axis_index("row")
    c = lax.axis_index("col")

    barrier = pltpu.get_barrier_semaphore()
    near = r + 1 - 2 * (r % 2)
    far_bit = r // (rows // 2)
    far = r + rows // 2 - rows * far_bit
    col_bit = c // (cols // 2)
    across = c + cols // 2 - cols * col_bit
    for step in range(1, rows):
        pl.semaphore_signal(
            barrier, inc=1, device_id=((r + step) % rows, c), device_id_type=MESH
        )
    pl.semaphore_signal(barrier, inc=1, device_id=(r, across), device_id_type=MESH)

    count = chunks // 2
    mid_lane = lanes // 2

    def place_weight(slot, top, bottom):
        size = 2 * order
        weight[slot, :, 0:size] = top
        weight[slot, :, size : 2 * size] = top
        weight[slot, :, 2 * size : 3 * size] = bottom

    def set_top(slot, source):
        place_weight(slot, *split(real_form(source[0], source[1])))

    def reorder_matrix():
        new = lax.broadcasted_iota(jnp.int32, (order, order), 0)
        old = lax.broadcasted_iota(jnp.int32, (order, order), 1)
        outer = new // low
        place = (new % low) * kk + 2 * (outer % chunks) + outer // chunks
        return (place == old).astype(F32).astype(BF16)

    def set_middle(slot, source):
        reorder = reorder_matrix()

        def moved(part):
            rows_moved = dot32(reorder, part).astype(BF16)
            return lax.dot_general(
                rows_moved, reorder, (((1,), (1,)), ((), ())), preferred_element_type=F32
            ).astype(BF16)

        real_parts = split(source[0])
        imag_parts = split(source[1])
        place_weight(
            slot,
            *(real_form(moved(re), moved(im)) for re, im in zip(real_parts, imag_parts)),
        )

    def crossed(first, second):
        return (
            jnp.concatenate([first[:, :mid_lane], second[:, :mid_lane]], axis=1),
            jnp.concatenate([first[:, mid_lane:], second[:, mid_lane:]], axis=1),
        )

    def apply(slot, value):
        top, bottom = split(value)
        return dot32(weight[slot], jnp.concatenate([top, bottom, top], axis=0))

    def put(i, result):
        state[2 * i] = result[:, :lanes].reshape(2, high, low, lanes)
        state[2 * i + 1] = result[:, lanes:].reshape(2, high, low, lanes)

    def get(i):
        return jnp.concatenate(
            [
                state[2 * i].reshape(2 * order, lanes),
                state[2 * i + 1].reshape(2 * order, lanes),
            ],
            axis=1,
        )

    def top_step(slot, i):
        put(i, apply(slot, get(i)))

    def each(h, step):
        def run(i, carry):
            step(i)
            return carry

        lax.fori_loop(h * count, (h + 1) * count, run, 0)

    def middle(slot, h):
        mine = slice(h * chunks, (h + 1) * chunks)

        def step(p, carry):
            columns = []
            for pair in range(2):
                pieces = []
                for d in range(2):
                    pieces += crossed(
                        state[mine, d, 4 * p + 2 * pair].reshape(chunks * low, lanes),
                        state[mine, d, 4 * p + 2 * pair + 1].reshape(chunks * low, lanes),
                    )
                columns.append(jnp.concatenate(pieces, axis=0))
            result = apply(slot, jnp.concatenate(columns, axis=1))
            for pair in range(2):
                piece = result[:, pair * lanes : (pair + 1) * lanes]
                for d in range(2):
                    start = d * order
                    both = crossed(
                        piece[start : start + chunks * low],
                        piece[start + chunks * low : start + order],
                    )
                    for own in range(2):
                        state[mine, d, 4 * p + 2 * pair + own] = both[own].reshape(
                            chunks, low, lanes
                        )
            return carry

        lax.fori_loop(0, high // 4, step, 0)

    def swap_copy(which, i, bit, device):
        return pltpu.make_async_remote_copy(
            src_ref=state.at[pl.ds(2 * i, 2), :, pl.ds((1 - bit) * half, half)],
            dst_ref=arrived.at[which, pl.ds(2 * i, 2)],
            send_sem=swap_send.at[which, i],
            recv_sem=swap_recv.at[which, i],
            device_id=device,
            device_id_type=MESH,
        )

    def swap_out(slot, h, which, bit, device):
        def send(i):
            top_step(slot, i)
            swap_copy(which, i, bit, device).start()

        each(h, send)

    def swap_in(slot, h, which, bit, device):
        def receive(i):
            swap_copy(which, i, bit, device).wait()
            state[pl.ds(2 * i, 2), :, pl.ds((1 - bit) * half, half)] = arrived[
                which, pl.ds(2 * i, 2)
            ]
            top_step(slot, i)

        each(h, receive)

    def lows(value):
        parts = jnp.concatenate([value[:order], value[order:]], axis=1)
        top, bottom = split(parts)
        joined = jnp.concatenate([top, bottom, top], axis=1)
        result = dot32(joined, low_weight[...])
        return jnp.concatenate([result[:, :lanes], result[:, lanes:]], axis=0)

    def gate(seg, number):
        return gates_ref.at[seg, number]

    set_top(0, gate(0, 0))

    def load(i, carry):
        value = jnp.concatenate(
            [
                amp_ref[pl.ds(2 * i, 2 * order, stride=kk), :],
                amp_ref[pl.ds(2 * i + 1, 2 * order, stride=kk), :],
            ],
            axis=1,
        )
        result = apply(0, value)
        both = crossed(result[:, :lanes], result[:, lanes:])
        for h in range(2):
            state[h * chunks + i] = both[h].reshape(2, high, low, lanes)
        return carry

    lax.fori_loop(0, chunks, load, 0)
    near_bit = r % 2
    set_middle(1, gate(0, 1))
    set_top(2, gate(0, 3))
    middle(1, 0)
    pl.semaphore_wait(barrier, rows)
    swap_out(2, 0, 0, near_bit, (near, c))
    middle(1, 1)
    swap_out(2, 1, 0, near_bit, (near, c))
    set_top(3, gate(1, 0))
    set_middle(4, gate(1, 1))
    set_top(5, gate(1, 3))
    for h in range(2):
        swap_in(3, h, 0, near_bit, (near, c))
        middle(4, h)
        swap_out(5, h, 1, far_bit, (far, c))

    set_top(6, gate(2, 0))
    set_middle(7, gate(2, 1))
    set_top(8, gate(2, 3))
    set_top(9, first_ref)
    for seg in range(3, 5):
        if seg > 3:
            set_top(3 * seg, gate(seg, 0))
        set_middle(3 * seg + 1, gate(seg, 1))
        set_top(3 * seg + 2, gate(seg, 3))
    merged = real_form_transposed(gates_ref[0, 2, 0], gates_ref[0, 2, 1])
    for seg in range(1, gates_ref.shape[0]):
        merged = product(
            merged, real_form_transposed(gates_ref[seg, 2, 0], gates_ref[seg, 2, 1])
        )
    top, bottom = split(merged)
    low_weight[0 : 2 * lanes] = top
    low_weight[2 * lanes : 4 * lanes] = top
    low_weight[4 * lanes : 6 * lanes] = bottom

    def map_copy(i, step):
        target = (r + step) % rows
        return pltpu.make_async_remote_copy(
            src_ref=stage.at[i, target],
            dst_ref=blocks.at[i, r],
            send_sem=map_send.at[i, step],
            recv_sem=map_recv.at[i, step],
            device_id=(target, c),
            device_id_type=MESH,
        )

    def map_out(i):
        result = apply(8, get(i))
        for own in range(2):
            for d in range(2):
                piece = result[
                    d * order : (d + 1) * order, own * lanes : (own + 1) * lanes
                ]
                if rest == 8:
                    stage[i, :, d, own * rest : (own + 1) * rest] = piece.reshape(
                        rows, rest, lanes
                    )
                else:
                    for t in range(rows):
                        stage[i, t, d, own * rest : (own + 1) * rest] = piece[
                            t * rest : (t + 1) * rest
                        ]
        for step in range(1, rows):
            map_copy(i, step).start()
        blocks[i, r] = stage[i, r]

    def map_in(i):
        for step in range(1, rows):
            map_copy(i, step).wait()
        columns = []
        for own in range(2):
            if rest == 8:
                pieces = [
                    blocks[i, :, d, own * rest : (own + 1) * rest].reshape(order, lanes)
                    for d in range(2)
                ]
            else:
                pieces = [
                    blocks[i, s, d, own * rest : (own + 1) * rest]
                    for d in range(2)
                    for s in range(rows)
                ]
            columns.append(jnp.concatenate(pieces, axis=0))
        put(i, apply(9, jnp.concatenate(columns, axis=1)))

    for h in range(2):
        swap_in(6, h, 1, far_bit, (far, c))
        middle(7, h)
        each(h, map_out)
    for h in range(2):
        each(h, map_in)
        middle(10, h)
        swap_out(11, h, 2, col_bit, (r, across))
    for h in range(2):
        swap_in(12, h, 2, col_bit, (r, across))
        middle(13, h)

    def finish(i, carry):
        value = jnp.concatenate(
            [state[h * chunks + i].reshape(2 * order, lanes) for h in range(2)], axis=1
        )
        result = apply(14, value)
        both = crossed(result[:, :lanes], result[:, lanes:])
        for own in range(2):
            out_ref[pl.ds(2 * i + own, 2 * order, stride=kk), :] = lows(both[own])
        return carry

    lax.fori_loop(0, chunks, finish, 0)


def body(amplitudes, gate_matrices, permutation):
    rows = lax.axis_size("row")
    cols = lax.axis_size("col")
    order = gate_matrices.shape[-1]
    amp_count = amplitudes.shape[-1]
    high = amp_count // (order * order)
    low = order // high
    kk = order // low
    rest = order // rows
    chunks = kk // 2
    chosen = (permutation[:, None] == jnp.arange(rows)[None, :]).astype(F32)
    first = jnp.einsum(
        "xjtw,ts->xjsw",
        gate_matrices[3, 0].reshape(2, order, rows, rest),
        chosen,
        precision=HIGHEST,
    ).reshape(2, order, order)
    vmem = pl.BlockSpec(memory_space=pltpu.VMEM)
    result = pl.pallas_call(
        functools.partial(kernel, rows, cols),
        out_shape=jax.ShapeDtypeStruct((2 * amp_count // order, order), F32),
        in_specs=[vmem] * 3,
        out_specs=vmem,
        scratch_shapes=[
            pltpu.VMEM((kk, 2, high, low, order), F32),
            pltpu.VMEM((15, 2 * order, 6 * order), BF16),
            pltpu.VMEM((6 * order, 2 * order), BF16),
            pltpu.VMEM((3, kk, 2, high // 2, low, order), F32),
            pltpu.VMEM((chunks, rows, 2, 2 * rest, order), F32),
            pltpu.VMEM((chunks, rows, 2, 2 * rest, order), F32),
            pltpu.SemaphoreType.DMA((3, chunks)),
            pltpu.SemaphoreType.DMA((3, chunks)),
            pltpu.SemaphoreType.DMA((chunks, rows)),
            pltpu.SemaphoreType.DMA((chunks, rows)),
        ],
        compiler_params=pltpu.CompilerParams(
            collective_id=0, has_side_effects=True, vmem_limit_bytes=48 * 2**20
        ),
    )(amplitudes.reshape(2 * amp_count // order, order), gate_matrices, first)
    return result.reshape(amplitudes.shape)


def solution(mesh):
    placed = (P(None, "row", "col", None), P(), P())
    return jax.shard_map(
        body, mesh=mesh, in_specs=placed, out_specs=P(None, "row", "col", None), check_vma=False
    )
```

time: 169 us -> 141 us (0.83)
  local copies, waits for them, and re-layouts: 24 us -> 4.05 us
  Pallas kernels: 145 us -> 135 us
    another operation x2 -> x0, local copies, waits for them, and re-layouts: 11.7 us -> none  [body(): mids = gate_matrices[:, 1].reshape(segs, 2, low, kk, low, kk)]
    pallas_call x1, Pallas kernels: 145 us -> 135 us  [body(): pl.pallas_call(functools.partial(kernel, rows, cols), out_shape=jax.Shape...]
    reshape x1 -> x0, local copies, waits for them, and re-layouts: 8.01 us -> none  [body(): mids = mids.transpose(0, 1, 3, 2, 5, 4).reshape(segs, 2, order, order)]
where the time goes in v3:
time: 141 us; the launch traced here: 140 us
  Pallas kernels  135 us (96%)
  local copies, waits for them, and re-layouts  4.05 us (3%)
    pallas_call x1, Pallas kernels, body(): pl.pallas_call(functools.partial(kernel, rows, cols), out_shape=jax.Shape...  135 us
    unnamed x4, local copies, waits for them, and re-layouts  3 us

profile of v3, /device:TPU:0, one launch (start us, length us, event | category | flops | bytes accessed | tf_op | source)
XLA Modules:
  0.0 140.4 jit_solution(5954278585909736214)
XLA Ops:
  0.0 0.9 slice.3
  0.9 0.1 copy.12
  1.0 0.9 convolution_bitcast_fusion
  1.9 0.1 copy.9.first_ref
  2.0 0.0 copy-start
  2.1 1.6 %copy-done = f32[2,1,1,262144]{3,2,1,0:T(1,128)S(1)} copy-done((f32[2,1,1,262144]{3,2,1,0:T(1,128)S(1)}, f32[2,1,1,262144]{3,2,1,0:T(1,128)}, u32[]{:S(2)}) %copy-start) | copy-done | bytes 2097176
  3.6 135.5 %shard_map.37 = f32[4096,128]{1,0:T(8,128)S(1)} custom-call(f32[4096,128]{1,0:T(8,128)S(1)} %bitcast.14, f32[5,4,2,128,128]{4,3,2,1,0:T(8,128)} %gates_ref.1, f32[2,128,128]{2,1,0:T(8,128)S(1)} %copy.9.first_ref), custom_call_target="tpu_custom_call" | custom-call | tf_op jit(solution)/shard_map/pallas_call | solution.py:374
  139.1 1.3 copy.18
  (1 shorter events, 0.0 us)
Async XLA Ops:
  2.0 1.6 %copy-start = (f32[2,1,1,262144]{3,2,1,0:T(1,128)S(1)}, f32[2,1,1,262144]{3,2,1,0:T(1,128)}, u32[]{:S(2)}) copy-start(f32[2,1,1,262144]{3,2,1,0:T(1,128)} %param.3) | copy-start | bytes 6291460

commit v4 on v3

--- a/solution.py
+++ b/solution.py
@@ -7,7 +7,6 @@
 from jax.experimental.pallas import tpu as pltpu
 from jax.sharding import PartitionSpec as P
 
-HIGHEST = lax.Precision.HIGHEST
 MESH = pl.DeviceIdType.MESH
 F32 = jnp.float32
 BF16 = jnp.bfloat16
@@ -58,7 +57,7 @@
     cols,
     amp_ref,
     gates_ref,
-    first_ref,
+    target_ref,
     out_ref,
     state,
     weight,
@@ -216,53 +215,60 @@
 
         each(h, receive)
 
-    def lows(value):
-        parts = jnp.concatenate([value[:order], value[order:]], axis=1)
-        top, bottom = split(parts)
-        joined = jnp.concatenate([top, bottom, top], axis=1)
-        result = dot32(joined, low_weight[...])
-        return jnp.concatenate([result[:, :lanes], result[:, lanes:]], axis=0)
-
     def gate(seg, number):
         return gates_ref.at[seg, number]
 
     set_top(0, gate(0, 0))
 
-    def load(i, carry):
-        value = jnp.concatenate(
-            [
-                amp_ref[pl.ds(2 * i, 2 * order, stride=kk), :],
-                amp_ref[pl.ds(2 * i + 1, 2 * order, stride=kk), :],
-            ],
-            axis=1,
-        )
-        result = apply(0, value)
-        both = crossed(result[:, :lanes], result[:, lanes:])
-        for h in range(2):
-            state[h * chunks + i] = both[h].reshape(2, high, low, lanes)
-        return carry
-
-    lax.fori_loop(0, chunks, load, 0)
+    def load(h):
+        def step(i):
+            columns = []
+            for own in range(2):
+                chunk = 2 * (i - h * count) + own
+                columns.append(
+                    crossed(
+                        amp_ref[pl.ds(2 * chunk, 2 * order, stride=kk), :],
+                        amp_ref[pl.ds(2 * chunk + 1, 2 * order, stride=kk), :],
+                    )[h]
+                )
+            put(i, apply(0, jnp.concatenate(columns, axis=1)))
+
+        each(h, step)
+
     near_bit = r % 2
+    load(0)
     set_middle(1, gate(0, 1))
+    middle(1, 0)
     set_top(2, gate(0, 3))
-    middle(1, 0)
     pl.semaphore_wait(barrier, rows)
     swap_out(2, 0, 0, near_bit, (near, c))
-    middle(1, 1)
-    swap_out(2, 1, 0, near_bit, (near, c))
     set_top(3, gate(1, 0))
     set_middle(4, gate(1, 1))
     set_top(5, gate(1, 3))
-    for h in range(2):
-        swap_in(3, h, 0, near_bit, (near, c))
-        middle(4, h)
-        swap_out(5, h, 1, far_bit, (far, c))
+    swap_in(3, 0, 0, near_bit, (near, c))
+    middle(4, 0)
+    swap_out(5, 0, 1, far_bit, (far, c))
+    load(1)
+    middle(1, 1)
+    swap_out(2, 1, 0, near_bit, (near, c))
+    swap_in(3, 1, 0, near_bit, (near, c))
+    middle(4, 1)
+    swap_out(5, 1, 1, far_bit, (far, c))
 
     set_top(6, gate(2, 0))
     set_middle(7, gate(2, 1))
     set_top(8, gate(2, 3))
-    set_top(9, first_ref)
+    chosen = (
+        target_ref[...] == lax.broadcasted_iota(jnp.int32, (order, order), 0)
+    ).astype(F32).astype(BF16)
+
+    def turned(part):
+        return lax.dot_general(
+            part, chosen, (((1,), (1,)), ((), ())), preferred_element_type=F32
+        ).astype(BF16)
+
+    parts = zip(split(gates_ref[3, 0, 0]), split(gates_ref[3, 0, 1]))
+    place_weight(9, *(real_form(turned(re), turned(im)) for re, im in parts))
     for seg in range(3, 5):
         if seg > 3:
             set_top(3 * seg, gate(seg, 0))
@@ -274,9 +280,15 @@
             merged, real_form_transposed(gates_ref[seg, 2, 0], gates_ref[seg, 2, 1])
         )
     top, bottom = split(merged)
-    low_weight[0 : 2 * lanes] = top
-    low_weight[2 * lanes : 4 * lanes] = top
-    low_weight[4 * lanes : 6 * lanes] = bottom
+    for h in range(2):
+        for place, part in enumerate((top, top, bottom)):
+            low_weight[h, place * lanes : (place + 1) * lanes] = jnp.concatenate(
+                [
+                    part[h * mid_lane : (h + 1) * mid_lane],
+                    part[lanes + h * mid_lane : lanes + (h + 1) * mid_lane],
+                ],
+                axis=0,
+            )
 
     def map_copy(i, step):
         target = (r + step) % rows
@@ -336,21 +348,31 @@
         each(h, map_in)
         middle(10, h)
         swap_out(11, h, 2, col_bit, (r, across))
+    def finish(h):
+        def step(i):
+            result = apply(14, get(i))
+            for own in range(2):
+                piece = result[:, own * lanes : (own + 1) * lanes]
+                both = crossed(piece[:order], piece[order:])
+                for odd in range(2):
+                    top, bottom = split(both[odd])
+                    share = dot32(
+                        jnp.concatenate([top, bottom, top], axis=1), low_weight[h]
+                    )
+                    k = 2 * (2 * (i - h * count) + own) + odd
+                    for d in range(2):
+                        where = pl.ds(d * order * kk + k, order, stride=kk)
+                        value = share[:, d * lanes : (d + 1) * lanes]
+                        if h:
+                            value = value + out_ref[where, :]
+                        out_ref[where, :] = value
+
+        each(h, step)
+
     for h in range(2):
         swap_in(12, h, 2, col_bit, (r, across))
         middle(13, h)
-
-    def finish(i, carry):
-        value = jnp.concatenate(
-            [state[h * chunks + i].reshape(2 * order, lanes) for h in range(2)], axis=1
-        )
-        result = apply(14, value)
-        both = crossed(result[:, :lanes], result[:, lanes:])
-        for own in range(2):
-            out_ref[pl.ds(2 * i + own, 2 * order, stride=kk), :] = lows(both[own])
-        return carry
-
-    lax.fori_loop(0, chunks, finish, 0)
+        finish(h)
 
 
 def body(amplitudes, gate_matrices, permutation):
@@ -363,13 +385,8 @@
     kk = order // low
     rest = order // rows
     chunks = kk // 2
-    chosen = (permutation[:, None] == jnp.arange(rows)[None, :]).astype(F32)
-    first = jnp.einsum(
-        "xjtw,ts->xjsw",
-        gate_matrices[3, 0].reshape(2, order, rows, rest),
-        chosen,
-        precision=HIGHEST,
-    ).reshape(2, order, order)
+    target = permutation[:, None] * rest + jnp.arange(rest, dtype=jnp.int32)[None, :]
+    target = target.reshape(1, order)
     vmem = pl.BlockSpec(memory_space=pltpu.VMEM)
     result = pl.pallas_call(
         functools.partial(kernel, rows, cols),
@@ -379,7 +396,7 @@
         scratch_shapes=[
             pltpu.VMEM((kk, 2, high, low, order), F32),
             pltpu.VMEM((15, 2 * order, 6 * order), BF16),
-            pltpu.VMEM((6 * order, 2 * order), BF16),
+            pltpu.VMEM((2, 3 * order, 2 * order), BF16),
             pltpu.VMEM((3, kk, 2, high // 2, low, order), F32),
             pltpu.VMEM((chunks, rows, 2, 2 * rest, order), F32),
             pltpu.VMEM((chunks, rows, 2, 2 * rest, order), F32),
@@ -391,7 +408,7 @@
         compiler_params=pltpu.CompilerParams(
             collective_id=0, has_side_effects=True, vmem_limit_bytes=48 * 2**20
         ),
-    )(amplitudes.reshape(2 * amp_count // order, order), gate_matrices, first)
+    )(amplitudes.reshape(2 * amp_count // order, order), gate_matrices, target)
     return result.reshape(amplitudes.shape)
 
 

time: 141 us -> 133 us (0.943)
  Pallas kernels: 135 us -> 129 us
    pallas_call x1, Pallas kernels: 135 us -> 129 us  [body(): pl.pallas_call(functools.partial(kernel, rows, cols), out_shape=jax.Shape...]
    unnamed x4 -> x3, local copies, waits for them, and re-layouts: 3 us -> 2.91 us
where the time goes in v4:
time: 133 us; the launch traced here: 132 us
  Pallas kernels  129 us (97%)
  local copies, waits for them, and re-layouts  3 us (2%)
    pallas_call x1, Pallas kernels, body(): pl.pallas_call(functools.partial(kernel, rows, cols), out_shape=jax.Shape...  129 us
    unnamed x3, local copies, waits for them, and re-layouts  2.91 us

profile of v4, /device:TPU:0, one launch (start us, length us, event | category | flops | bytes accessed | tf_op | source)
XLA Modules:
  0.0 132.3 jit_solution(11880398113243707881)
XLA Ops:
  0.0 0.7 broadcast_multiply_fusion
  0.7 0.1 iota_add_fusion
  0.7 0.1 add.26.target_ref
  0.8 0.0 copy-start
  0.8 1.6 %copy-done = f32[2,1,1,262144]{3,2,1,0:T(1,128)S(1)} copy-done((f32[2,1,1,262144]{3,2,1,0:T(1,128)S(1)}, f32[2,1,1,262144]{3,2,1,0:T(1,128)}, u32[]{:S(2)}) %copy-start) | copy-done | bytes 2097176
  2.4 128.6 %shard_map.37 = f32[4096,128]{1,0:T(8,128)S(1)} custom-call(f32[4096,128]{1,0:T(8,128)S(1)} %bitcast.3, f32[5,4,2,128,128]{4,3,2,1,0:T(8,128)} %gates_ref.1, s32[1,128]{1,0:T(1,128)S(1)} %add.26.target_ref), custom_call_target="tpu_custom_call" | custom-call | tf_op jit(solution)/shard_map/pallas_call | solution.py:391
  131.0 1.3 copy.7
Async XLA Ops:
  0.8 1.6 %copy-start = (f32[2,1,1,262144]{3,2,1,0:T(1,128)S(1)}, f32[2,1,1,262144]{3,2,1,0:T(1,128)}, u32[]{:S(2)}) copy-start(f32[2,1,1,262144]{3,2,1,0:T(1,128)} %param.3) | copy-start | bytes 6291460

commit v5 on v4

--- a/solution.py
+++ b/solution.py
@@ -151,12 +151,12 @@
     def top_step(slot, i):
         put(i, apply(slot, get(i)))
 
-    def each(h, step):
+    def each(h, step, unroll=4):
         def run(i, carry):
             step(i)
             return carry
 
-        lax.fori_loop(h * count, (h + 1) * count, run, 0)
+        lax.fori_loop(h * count, (h + 1) * count, run, 0, unroll=unroll)
 
     def middle(slot, h):
         mine = slice(h * chunks, (h + 1) * chunks)
@@ -186,7 +186,7 @@
                         )
             return carry
 
-        lax.fori_loop(0, high // 4, step, 0)
+        lax.fori_loop(0, high // 4, step, 0, unroll=4)
 
     def swap_copy(which, i, bit, device):
         return pltpu.make_async_remote_copy(
@@ -343,9 +343,9 @@
     for h in range(2):
         swap_in(6, h, 1, far_bit, (far, c))
         middle(7, h)
-        each(h, map_out)
+        each(h, map_out, 1)
     for h in range(2):
-        each(h, map_in)
+        each(h, map_in, 1)
         middle(10, h)
         swap_out(11, h, 2, col_bit, (r, across))
     def finish(h):

time: 133 us -> 128 us (0.962)
  Pallas kernels: 129 us -> 124 us
    pallas_call x1, Pallas kernels: 129 us -> 124 us  [body(): pl.pallas_call(functools.partial(kernel, rows, cols), out_shape=jax.Shape...]
where the time goes in v5:
time: 128 us
  Pallas kernels  124 us (97%)
  local copies, waits for them, and re-layouts  3 us (2%)
    pallas_call x1, Pallas kernels, body(): pl.pallas_call(functools.partial(kernel, rows, cols), out_shape=jax.Shape...  124 us
    unnamed x3, local copies, waits for them, and re-layouts  2.91 us

profile of v5, /device:TPU:0, one launch (start us, length us, event | category | flops | bytes accessed | tf_op | source)
XLA Modules:
  0.0 127.9 jit_solution(1340860002397414178)
XLA Ops:
  0.0 0.7 broadcast_multiply_fusion
  0.7 0.1 iota_add_fusion
  0.7 0.1 add.26.target_ref
  0.8 0.0 copy-start
  0.8 1.6 %copy-done = f32[2,1,1,262144]{3,2,1,0:T(1,128)S(1)} copy-done((f32[2,1,1,262144]{3,2,1,0:T(1,128)S(1)}, f32[2,1,1,262144]{3,2,1,0:T(1,128)}, u32[]{:S(2)}) %copy-start) | copy-done | bytes 2097176
  2.4 124.1 %shard_map.37 = f32[4096,128]{1,0:T(8,128)S(1)} custom-call(f32[4096,128]{1,0:T(8,128)S(1)} %bitcast.3, f32[5,4,2,128,128]{4,3,2,1,0:T(8,128)} %gates_ref.1, s32[1,128]{1,0:T(1,128)S(1)} %add.26.target_ref), custom_call_target="tpu_custom_call" | custom-call | tf_op jit(solution)/shard_map/pallas_call | solution.py:391
  126.6 1.3 %copy.7 = f32[2,1,1,262144]{3,2,1,0:T(1,128)} copy(f32[2,1,1,262144]{3,2,1,0:T(1,128)S(1)} %bitcast.2) | data formatting | bytes 4194304
Async XLA Ops:
  0.8 1.6 %copy-start = (f32[2,1,1,262144]{3,2,1,0:T(1,128)S(1)}, f32[2,1,1,262144]{3,2,1,0:T(1,128)}, u32[]{:S(2)}) copy-start(f32[2,1,1,262144]{3,2,1,0:T(1,128)} %param.3) | copy-start | bytes 6291460
